TPU v7x, 32 devices: a whole 2x2x4 slice. The times are simulated.
32 devices in a mesh: dp: 16 (over z, y, x), tensor: 2 (over core).
Axes of the slice: x: 2, y: 2, z: 4, core: 2. Of those that a mesh axis runs over, the one named last changes fastest.
Arguments:
- fc_grads: bfloat16 [16, 768, 3072], P('dp', None, 'tensor')
- fc_error: bfloat16 [16, 768, 3072], P('dp', None, 'tensor'), may hold values from -4 to 4
- query: float32 [3072, 32], P('tensor'), may hold values from -0.109375 to 0.109375
- gram_inverse: float32 [32, 32], replicated
- fc_master: float32 [768, 3072], P('dp', 'tensor'), may hold values from -6 to 6
- fc_momentum: float32 [768, 3072], P('dp', 'tensor'), may hold values from -3 to 3
- vec_grads: bfloat16 [16, 5376], P('dp'), may hold values from -6 to 6
- vec_master: float32 [5376], P('dp'), may hold values from -6 to 6
- vec_momentum: float32 [5376], P('dp'), may hold values from -4 to 4
Outputs:
- new_error: bfloat16 [16, 768, 3072], P('dp', None, 'tensor')
- new_momentum: float32 [768, 3072], P('dp', 'tensor')
- new_master: float32 [768, 3072], P('dp', 'tensor')
- new_weights: bfloat16 [768, 3072], P(None, 'tensor')
- vec_new_momentum: float32 [5376], P('dp')
- vec_new_master: float32 [5376], P('dp')
- vec_weights: bfloat16 [5376], replicated
All inputs are finite; a program needn't handle non-finite values.
Results may differ from a plain program's by a relative error of at most 0.0085.
Values may be sent and summed in bfloat16 or wider, within the bound.
A program may use at most 64 MiB of HBM per device.

v0:
```python
import jax
import jax.numpy as jnp
from jax import lax
from jax.sharding import PartitionSpec as P

momentum_decay = 0.9
step_size = 0.5


def on_device(
    fc_grads,
    fc_error,
    query,
    gram_inverse,
    fc_master,
    fc_momentum,
    vec_grads,
    vec_master,
    vec_momentum,
):
    replicas = lax.axis_size("dp")
    replica_index = lax.axis_index("dp")
    merged = (fc_grads[0].astype(jnp.float32) + fc_error[0].astype(jnp.float32)).astype(
        jnp.bfloat16
    )
    query_b = query.astype(jnp.bfloat16)
    row_part = jnp.dot(merged, query_b, preferred_element_type=jnp.float32)
    vec_term = vec_grads[0].astype(jnp.float32)
    shard_len = vec_master.shape[0]
    row_total = lax.psum(row_part, ("dp", "tensor"))
    vec_total = lax.psum(vec_term, "dp")
    vec_mean = (
        lax.dynamic_slice_in_dim(vec_total, replica_index * shard_len, shard_len, 0) / replicas
    )
    row_mean = row_total / replicas
    row_basis = jnp.dot(row_mean, gram_inverse, precision=lax.Precision.HIGHEST)
    basis_b = row_basis.astype(jnp.bfloat16)
    col_part = lax.dot_general(
        merged, basis_b, (((0,), (0,)), ((), ())), preferred_element_type=jnp.float32
    )
    col_mean = lax.psum(col_part, "dp") / replicas
    approx = jnp.dot(row_basis, col_mean.T, precision=lax.Precision.HIGHEST)
    new_error = (merged.astype(jnp.float32) - approx).astype(jnp.bfloat16)[None]
    state_rows = fc_master.shape[0]
    basis_rows = lax.dynamic_slice_in_dim(row_basis, replica_index * state_rows, state_rows, 0)
    approx_rows = jnp.dot(basis_rows, col_mean.T, precision=lax.Precision.HIGHEST)
    new_momentum = momentum_decay * fc_momentum + approx_rows
    new_master = fc_master - step_size * (approx_rows + momentum_decay * new_momentum)
    vec_new_momentum = momentum_decay * vec_momentum + vec_mean
    vec_new_master = vec_master - step_size * (vec_mean + momentum_decay * vec_new_momentum)
    new_weights, vec_weights = (
        lax.all_gather(new_master.astype(jnp.bfloat16), "dp", axis=0, tiled=True),
        lax.all_gather(vec_new_master.astype(jnp.bfloat16), "dp", axis=0, tiled=True),
    )
    return (
        new_error,
        new_momentum,
        new_master,
        new_weights,
        vec_new_momentum,
        vec_new_master,
        vec_weights,
    )


def solution(mesh):
    return jax.shard_map(
        on_device,
        mesh=mesh,
        in_specs=(
            P("dp", None, "tensor"),
            P("dp", None, "tensor"),
            P("tensor", None),
            P(),
            P("dp", "tensor"),
            P("dp", "tensor"),
            P("dp", None),
            P("dp"),
            P("dp"),
        ),
        out_specs=(
            P("dp", None, "tensor"),
            P("dp", "tensor"),
            P("dp", "tensor"),
            P(None, "tensor"),
            P("dp"),
            P("dp"),
            P(),
        ),
        check_vma=False,
    )
```

profile of v0, /device:TPU:0, one launch (start us, length us, event | category | flops | bytes accessed | tf_op | source)
XLA Modules:
  0.0 424.8 jit_solution(2029366436794385196)
XLA Ops:
  7.2 0.0 copy-start
  7.2 0.0 copy-start.1
  7.2 0.0 all-reduce.4.cloned.1.call-start
  7.2 4.0 fusion.10
  11.3 0.0 all-reduce.4.cloned.1.call-update
  11.3 0.0 all-reduce.6.cloned.1.call-start
  11.3 132.8 %all-reduce.4.cloned.1.call-done = f32[768,32]{1,0:T(8,128)} async-done(((f32[768,32]{1,0:T(8,128)}), f32[768,32]{1,0:T(8,128)}) %all-reduce.4.cloned.1.call-update) | async-done | bytes 98320 | tf_op jit(solution)/shard_map/psum | solution.py:30
  144.1 0.0 copy-done
  144.1 1.5 fusion.2
  145.6 0.0 copy-done.1
  145.6 0.0 copy-start.2
  145.7 0.0 copy-start.3
  145.7 0.0 copy-start.7
  145.7 0.0 copy-start.4
  145.7 0.0 copy-start.5
  145.7 0.0 copy-start.6
  145.7 3.1 fusion.12
  148.8 0.0 all-reduce.6.cloned.1.call-update
  148.9 0.0 all-gather.2.cloned.1.call-start
  148.9 107.7 %all-reduce.6.cloned.1.call-done = f32[1536,32]{0,1:T(8,128)} async-done(((f32[1536,32]{0,1:T(8,128)}), f32[1536,32]{0,1:T(8,128)}) %all-reduce.6.cloned.1.call-update) | async-done | bytes 196624 | tf_op jit(solution)/shard_map/psum | solution.py:41
  256.6 0.0 copy-done.2
  256.6 0.0 copy-done.3
  256.6 2.3 fusion.22
  259.0 0.0 all-gather.2.cloned.1.call-update
  259.0 0.0 copy-done.7
  259.0 0.6 dynamic-slice
  260.2 0.0 copy-done.4
  260.3 0.1 convert_reduce_fusion
  260.3 75.4 %psum.23 = f32[5376]{0:T(1024)S(1)} all-reduce(f32[5376]{0:T(1024)S(1)} %convert_reduce_fusion), channel_id=1, replica_groups=mesh['dp'=16,'tensor'=2] {'dp'}, use_global_device_ids=true, to_apply=%region_2.0 | all-reduce | flops 5376 | bytes 43008 | tf_op jit(solution)/shard_map/psum | solution.py:31
  335.8 0.0 copy-done.5
  335.8 0.0 copy-done.6
  335.8 0.7 fusion.21
  336.4 0.2 dynamic-update-slice
  336.6 71.8 %all-reduce = bf16[5376]{0:T(1024)(128)(2,1)} all-reduce(bf16[5376]{0:T(1024)(128)(2,1)S(1)} %dynamic-update-slice), channel_id=1, replica_groups=mesh['dp'=16,'tensor'=2] {'dp'}, use_global_device_ids=true, to_apply=%add | all-reduce | flops 5376 | bytes 21504
  408.4 6.6 %fusion = bf16[1,768,1536]{2,1,0:T(8,128)(2,1)} fusion(f32[768,32]{0,1:T(8,128)S(1)} %fusion.2, f32[1536,32]{0,1:T(8,128)} %all-reduce.6.cloned.1.call-done, bf16[1,768,1536]{2,1,0:T(8,128)(2,1)S(1)} %copy-done.1, bf16[1,768,1536]{2,1,0:T(8,128)(2,1)} %param.9), kind=kOutput, calls=%fused_computation.2 | convolution fusion | flops 461291520 | bytes 7372800 | tf_op jit(solution)/shard_map/dot_general | solution.py:42
  415.0 0.0 all-gather.2.cloned.1.call-done
  415.0 3.2 copy.20
  (1 shorter events, 0.0 us)
Async XLA Ops:
  7.2 136.9 %copy-start = (f32[32,32]{1,0:T(8,128)S(1)}, f32[32,32]{1,0:T(8,128)}, u32[]{:S(2)}) copy-start(f32[32,32]{1,0:T(8,128)} %param.12) | copy-start | bytes 12292
  7.2 138.5 %copy-start.1 = (bf16[1,768,1536]{2,1,0:T(8,128)(2,1)S(1)}, bf16[1,768,1536]{2,1,0:T(8,128)(2,1)}, u32[]{:S(2)}) copy-start(bf16[1,768,1536]{2,1,0:T(8,128)(2,1)} %param.10) | copy-start | bytes 7077892
  7.2 136.9 %all-reduce.4.cloned.1.call-start = ((), (), s32[]{:S(2)}) async-start(), calls=%async_computation | async-start | bytes 786432 | tf_op jit(solution)/shard_map/psum | solution.py:30
  11.3 245.3 %all-reduce.6.cloned.1.call-start = ((), (), s32[]{:S(2)}) async-start(), calls=%async_computation.1 | async-start | bytes 393216 | tf_op jit(solution)/shard_map/psum | solution.py:41
  145.6 111.0 %copy-start.2 = (f32[48,1536]{1,0:T(8,128)S(1)}, f32[48,1536]{1,0:T(8,128)}, u32[]{:S(2)}) copy-start(f32[48,1536]{1,0:T(8,128)} %param.13) | copy-start | bytes 884740
  145.7 111.0 %copy-start.3 = (f32[48,1536]{1,0:T(8,128)S(1)}, f32[48,1536]{1,0:T(8,128)}, u32[]{:S(2)}) copy-start(f32[48,1536]{1,0:T(8,128)} %param.14) | copy-start | bytes 884740
  145.7 113.3 %copy-start.7 = (u32[32]{0:T(128)S(1)}, u32[32]{0:T(128)}, u32[]{:S(2)}) copy-start(u32[32]{0:T(128)} %constant.34) | copy-start | bytes 388
  145.7 114.6 %copy-start.4 = (bf16[1,5376]{1,0:T(2,128)(2,1)S(1)}, bf16[1,5376]{1,0:T(2,128)(2,1)}, u32[]{:S(2)}) copy-start(bf16[1,5376]{1,0:T(2,128)(2,1)} %param.15) | copy-start | bytes 32260
  145.7 190.1 %copy-start.5 = (f32[336]{0:T(512)S(1)}, f32[336]{0:T(512)}, u32[]{:S(2)}) copy-start(f32[336]{0:T(512)} %param.16) | copy-start | bytes 4036
  145.7 190.1 %copy-start.6 = (f32[336]{0:T(512)S(1)}, f32[336]{0:T(512)}, u32[]{:S(2)}) copy-start(f32[336]{0:T(512)} %param.17) | copy-start | bytes 4036
  148.9 266.2 %all-gather.2.cloned.1.call-start = ((), (), s32[]{:S(2)}) async-start(), calls=%async_computation.2 | async-start | bytes 2506752 | tf_op jit(solution)/shard_map/all_gather | solution.py:52
Sparse Core Ops, SparseCore 0:
  13.9 130.1 all-reduce.3
  150.8 105.8 all-reduce.5
  260.0 61.8 all-gather.1
where the time goes:
time: 425 us
  waiting for transfers between devices  241 us (57%)
  blocking collectives  147 us (35%)
  matrix products  17.6 us (4%)
  between operations  14.5 us (3%)
    psum x1, waiting for transfers between devices, on_device(): row_total = lax.psum(row_part, ('dp', 'tensor'))  133 us
    psum x1, waiting for transfers between devices, on_device(): col_mean = lax.psum(col_part, 'dp') / replicas  108 us
    psum x1, blocking collectives, on_device(): vec_total = lax.psum(vec_term, 'dp')  75.4 us
    unnamed x1, blocking collectives  71.8 us
  transfers between devices with their start and end apart: 3, of which 2 were waited for; matrix products, arithmetic and copies ran while one was open for 2% of the time, Pallas kernels for 0%

commit v1 on v0

v1 whole, which is shorter than its diff:
```python
import functools

import jax
import jax.numpy as jnp
from jax import lax
from jax.experimental import pallas as pl
from jax.experimental.pallas import tpu as pltpu
from jax.sharding import PartitionSpec as P

momentum_decay = 0.9
step_size = 0.5
base_decay = step_size * momentum_decay * momentum_decay
approx_scale = step_size * (1.0 + momentum_decay)

MESH = pl.DeviceIdType.MESH
INNER = 4
ROW_BLOCK = 128
COL_OWNERS = 16
VMEM_LIMIT = 40 * 1024 * 1024


def remote(src, dst, send_sem, recv_sem, dp, core):
    return pltpu.make_async_remote_copy(
        src_ref=src,
        dst_ref=dst,
        send_sem=send_sem,
        recv_sem=recv_sem,
        device_id=(dp, core),
        device_id_type=MESH,
    )


def wait_bytes(ref, sem):
    pltpu.make_async_copy(ref, ref, sem).wait()


def exchange_kernel(
    n,
    cores,
    grads,
    error,
    query,
    gram,
    vec_in,
    master,
    momentum,
    merged_out,
    base_all,
    basis_out,
    col_out,
    vec_out,
    grads_v,
    error_v,
    merged,
    own_base,
    part,
    part_in,
    total,
    col_part,
    col_in,
    col_total,
    load_sem,
    out_sem,
    part_send,
    part_recv,
    total_send,
    total_recv,
    cpart_send,
    cpart_recv,
    ctotal_send,
    ctotal_recv,
    base_send,
    line_recv,
    plane_recv,
):
    rows_all, columns = merged.shape
    blocks = rows_all // ROW_BLOCK
    row_chunks = 2 * blocks
    chunks = part.shape[0]
    devices = n * cores
    me, core = lax.axis_index("dp"), lax.axis_index("tensor")
    flat = core * n + me
    outer = n // INNER
    o, i = lax.div(me, INNER), lax.rem(me, INNER)

    def load(b):
        rows = pl.ds(pl.multiple_of(b * ROW_BLOCK, ROW_BLOCK), ROW_BLOCK)
        return (
            pltpu.make_async_copy(grads.at[0, rows], grads_v.at[rows], load_sem.at[b, 0]),
            pltpu.make_async_copy(error.at[0, rows], error_v.at[rows], load_sem.at[b, 1]),
        )

    for b in range(blocks):
        for copy in load(b):
            copy.start()

    barrier = pltpu.get_barrier_semaphore()

    def greet(t, carry):
        f = lax.rem(flat + t, devices)
        pl.semaphore_signal(
            barrier, inc=1, device_id=(lax.rem(f, n), lax.div(f, n)), device_id_type=MESH
        )
        return carry

    lax.fori_loop(1, devices, greet, 0)

    own_base[...] = (master[...] - base_decay * momentum[...]).astype(jnp.bfloat16)
    query_t = query[...].T.astype(jnp.bfloat16)
    part[row_chunks:] = vec_in[...]

    pl.semaphore_wait(barrier, devices - 1)

    keep = pltpu.make_async_copy(own_base, base_all.at[me], out_sem.at[0])
    keep.start()

    def send_line(t, carry):
        o2 = lax.rem(o + t, outer)
        remote(
            own_base, base_all.at[me], base_send, line_recv.at[o], o2 * INNER + i, core
        ).start()
        return carry

    lax.fori_loop(1, outer, send_line, 0)

    def send_plane(s, carry):
        i2 = lax.rem(i + s, INNER)
        remote(own_base, base_all.at[me], base_send, plane_recv, o * INNER + i2, core).start()
        return carry

    lax.fori_loop(1, INNER, send_plane, 0)

    def send_part(k):
        mine = flat == k

        @pl.when(mine)
        def _():
            part_in[pl.ds(flat, 1)] = part[pl.ds(k, 1)]

        @pl.when(jnp.logical_not(mine))
        def _():
            remote(
                part.at[k], part_in.at[flat], part_send, part_recv, lax.rem(k, n), lax.div(k, n)
            ).start()

    def send_vec(k, carry):
        send_part(k)
        return carry

    lax.fori_loop(row_chunks, chunks, send_vec, 0)

    def row_step(b, carry):
        for copy in load(b):
            copy.wait()
        rows = pl.ds(pl.multiple_of(b * ROW_BLOCK, ROW_BLOCK), ROW_BLOCK)
        block = (
            grads_v[rows, :].astype(jnp.float32) + error_v[rows, :].astype(jnp.float32)
        ).astype(jnp.bfloat16)
        merged[rows, :] = block
        term = lax.dot_general(
            query_t, block, (((1,), (1,)), ((), ())), preferred_element_type=jnp.float32
        )
        part[pl.ds(2 * b, 1)] = term[None, :16]
        part[pl.ds(2 * b + 1, 1)] = term[None, 16:]
        send_part(2 * b)
        send_part(2 * b + 1)
        return carry

    lax.fori_loop(0, blocks, row_step, 0)
    keep_merged = pltpu.make_async_copy(merged, merged_out, out_sem.at[1])
    keep_merged.start()

    owner = flat < chunks

    @pl.when(owner)
    def _():
        wait_bytes(part_in.at[pl.ds(0, devices - 1)], part_recv)
        total[pl.ds(flat, 1)] = jnp.sum(part_in[...], axis=0)[None]

        def spread(t, carry):
            f = lax.rem(flat + t, devices)
            remote(
                total.at[flat],
                total.at[flat],
                total_send,
                total_recv,
                lax.rem(f, n),
                lax.div(f, n),
            ).start()
            return carry

        lax.fori_loop(1, devices, spread, 0)
        wait_bytes(total.at[pl.ds(0, chunks - 1)], total_recv)

    @pl.when(jnp.logical_not(owner))
    def _():
        wait_bytes(total.at[pl.ds(0, chunks)], total_recv)

    row_mean = (
        jnp.concatenate(
            [
                jnp.concatenate([total[2 * b], total[2 * b + 1]], axis=0)
                for b in range(blocks)
            ],
            axis=1,
        )
        / n
    )
    basis = jnp.dot(
        gram[...].T,
        row_mean,
        precision=lax.Precision.HIGHEST,
        preferred_element_type=jnp.float32,
    )
    basis_b = basis.astype(jnp.bfloat16)

    wide = columns // 4
    for c in range(4):
        term = jnp.dot(
            basis_b, merged[:, c * wide : (c + 1) * wide], preferred_element_type=jnp.float32
        )
        for r in range(4):
            k = 4 * c + r
            col_part[k] = term[8 * r : 8 * r + 8]
        for r in range(4):
            k = 4 * c + r

            @pl.when(me == k)
            def _(k=k):
                col_in[pl.ds(me, 1)] = col_part[pl.ds(k, 1)]

            @pl.when(me != k)
            def _(k=k):
                remote(
                    col_part.at[k], col_in.at[me], cpart_send, cpart_recv, k, core
                ).start()

    def relay(t, carry):
        o2 = lax.rem(o + outer - t, outer)
        slot = o2 * INNER + i
        wait_bytes(base_all.at[slot], line_recv.at[o2])

        def hand(s, inner_carry):
            i2 = lax.rem(i + s, INNER)
            remote(
                base_all.at[slot],
                base_all.at[slot],
                base_send,
                plane_recv,
                o * INNER + i2,
                core,
            ).start()
            return inner_carry

        return lax.fori_loop(1, INNER, hand, carry)

    lax.fori_loop(1, outer, relay, 0)

    high = basis_b.astype(jnp.float32)
    low = basis - high
    basis_out[...] = jnp.concatenate([high, low, high, low], axis=0).T.astype(jnp.bfloat16)
    vec_out[...] = total[row_chunks:]

    def col_owner():
        wait_bytes(col_in.at[pl.ds(0, n - 1)], cpart_recv)
        col_total[pl.ds(me, 1)] = jnp.sum(col_in[...], axis=0)[None]

        def spread(t, carry):
            remote(
                col_total.at[me],
                col_total.at[me],
                ctotal_send,
                ctotal_recv,
                lax.rem(me + t, n),
                core,
            ).start()
            return carry

        lax.fori_loop(1, n, spread, 0)
        wait_bytes(col_total.at[pl.ds(0, COL_OWNERS - 1)], ctotal_recv)

    if n == COL_OWNERS:
        col_owner()
    else:
        pl.when(me < COL_OWNERS)(col_owner)

        @pl.when(me >= COL_OWNERS)
        def _():
            wait_bytes(col_total.at[pl.ds(0, COL_OWNERS)], ctotal_recv)

    for c in range(4):
        col_mean = jnp.concatenate([col_total[4 * c + r] for r in range(4)], axis=0) / n
        col_high = col_mean.astype(jnp.bfloat16)
        col_low = (col_mean - col_high.astype(jnp.float32)).astype(jnp.bfloat16)
        col_out[:, c * wide : (c + 1) * wide] = jnp.concatenate(
            [col_high, col_high, col_low, col_low], axis=0
        )

    keep.wait()
    keep_merged.wait()

    @pl.when(owner)
    def _():
        wait_bytes(part.at[pl.ds(0, chunks - 1)], part_send)
        wait_bytes(part_in.at[pl.ds(0, devices - 1)], total_send)

    @pl.when(jnp.logical_not(owner))
    def _():
        wait_bytes(part.at[pl.ds(0, chunks)], part_send)

    def col_sent():
        wait_bytes(col_part.at[pl.ds(0, COL_OWNERS - 1)], cpart_send)
        wait_bytes(col_in.at[pl.ds(0, n - 1)], ctotal_send)

    if n == COL_OWNERS:
        col_sent()
    else:
        pl.when(me < COL_OWNERS)(col_sent)

        @pl.when(me >= COL_OWNERS)
        def _():
            wait_bytes(col_part.at[pl.ds(0, COL_OWNERS)], cpart_send)

    wait_bytes(base_all.at[pl.ds(0, (INNER - 1) * outer)], plane_recv)
    wait_bytes(base_all.at[pl.ds(0, n - 1)], base_send)


def exchange(n, cores, grads, error, query, gram, vec_in, master, momentum):
    rows_all, columns = grads.shape[1:]
    rank = query.shape[1]
    rows = master.shape[0]
    blocks = rows_all // ROW_BLOCK
    chunks = 2 * blocks + vec_in.shape[0]
    wide = columns // 4
    devices = n * cores
    vmem = pl.BlockSpec(memory_space=pltpu.VMEM)
    hbm = pl.BlockSpec(memory_space=pl.ANY)
    dma = pltpu.SemaphoreType.DMA
    f32, bf16 = jnp.float32, jnp.bfloat16
    return pl.pallas_call(
        functools.partial(exchange_kernel, n, cores),
        out_shape=(
            jax.ShapeDtypeStruct((rows_all, columns), bf16),
            jax.ShapeDtypeStruct((n, rows, columns), bf16),
            jax.ShapeDtypeStruct((rows_all, 4 * rank), bf16),
            jax.ShapeDtypeStruct((4 * rank, columns), bf16),
            jax.ShapeDtypeStruct(vec_in.shape, f32),
        ),
        in_specs=[hbm, hbm, vmem, vmem, vmem, vmem, vmem],
        out_specs=(hbm, hbm, vmem, vmem, vmem),
        scratch_shapes=[
            pltpu.VMEM((rows_all, columns), bf16),
            pltpu.VMEM((rows_all, columns), bf16),
            pltpu.VMEM((rows_all, columns), bf16),
            pltpu.VMEM((rows, columns), bf16),
            pltpu.VMEM((chunks, 16, 128), f32),
            pltpu.VMEM((devices, 16, 128), f32),
            pltpu.VMEM((chunks, 16, 128), f32),
            pltpu.VMEM((COL_OWNERS, 8, wide), f32),
            pltpu.VMEM((n, 8, wide), f32),
            pltpu.VMEM((COL_OWNERS, 8, wide), f32),
            dma((blocks, 2)),
            dma((2,)),
        ]
        + [dma] * 8
        + [dma, dma((n // INNER,)), dma],
        compiler_params=pltpu.CompilerParams(
            collective_id=0, has_side_effects=True, vmem_limit_bytes=VMEM_LIMIT
        ),
        cost_estimate=pl.CostEstimate(
            flops=4 * rows_all * columns * rank, bytes_accessed=14000000, transcendentals=0
        ),
        name="exchange",
    )(grads, error, query, gram, vec_in, master, momentum)


def update_kernel(
    rows_step,
    merged,
    base,
    basis,
    col,
    master,
    momentum,
    new_error,
    new_momentum,
    new_master,
    new_weights,
):
    step = pl.program_id(0)
    here = pl.ds(pl.multiple_of(step * rows_step, rows_step), rows_step)
    approx = jnp.dot(basis[here, :], col[...], preferred_element_type=jnp.float32)
    new_error[...] = (merged[...].astype(jnp.float32) - approx).astype(jnp.bfloat16)
    new_weights[...] = (base[...].astype(jnp.float32) - approx_scale * approx).astype(
        jnp.bfloat16
    )

    @pl.when(step == 0)
    def _():
        rows, rows_all = master.shape[0], basis.shape[0]
        first = lax.axis_index("dp") * rows
        shape = (rows, rows_all)
        chosen = lax.broadcasted_iota(jnp.int32, shape, 1) == first + lax.broadcasted_iota(
            jnp.int32, shape, 0
        )
        basis_rows = jnp.dot(
            chosen.astype(jnp.float32).astype(jnp.bfloat16),
            basis[...],
            preferred_element_type=jnp.float32,
        ).astype(jnp.bfloat16)
        approx_rows = jnp.dot(basis_rows, col[...], preferred_element_type=jnp.float32)
        moved = momentum_decay * momentum[...] + approx_rows
        new_momentum[...] = moved
        new_master[...] = master[...] - step_size * (approx_rows + momentum_decay * moved)


def update(merged, base, basis, col, master, momentum):
    rows_all, columns = merged.shape
    steps = 6
    rows_step = rows_all // steps
    tile = pl.BlockSpec((rows_step, columns), lambda s: (s, 0))

    def whole(x):
        return pl.BlockSpec(x.shape, lambda s: (0, 0))

    state = jax.ShapeDtypeStruct(master.shape, jnp.float32)
    return pl.pallas_call(
        functools.partial(update_kernel, rows_step),
        grid=(steps,),
        out_shape=(
            jax.ShapeDtypeStruct((1, rows_all, columns), jnp.bfloat16),
            state,
            state,
            jax.ShapeDtypeStruct((rows_all, columns), jnp.bfloat16),
        ),
        in_specs=[tile, tile, whole(basis), whole(col), whole(master), whole(momentum)],
        out_specs=(
            pl.BlockSpec((None, rows_step, columns), lambda s: (0, s, 0)),
            whole(master),
            whole(master),
            tile,
        ),
        compiler_params=pltpu.CompilerParams(vmem_limit_bytes=VMEM_LIMIT),
        name="update",
    )(merged, base, basis, col, master, momentum)


def on_device(
    n,
    cores,
    fc_grads,
    fc_error,
    query,
    gram_inverse,
    fc_master,
    fc_momentum,
    vec_grads,
    vec_master,
    vec_momentum,
):
    replica = lax.axis_index("dp")
    length, shard = vec_grads.shape[1], vec_master.shape[0]
    counts = (lax.axis_index("tensor") == 0).astype(jnp.float32)
    padded = -(-length // 2048) * 2048
    vec_base = lax.dynamic_update_slice_in_dim(
        jnp.zeros((padded,), jnp.float32),
        vec_master - base_decay * vec_momentum,
        replica * shard,
        0,
    )
    vec_sum = jnp.pad(vec_grads[0].astype(jnp.float32), (0, padded - length))
    vec_in = (counts * jnp.concatenate([vec_sum, vec_base])).reshape(-1, 16, 128)

    merged, base, basis, col, vec_out = exchange(
        n, cores, fc_grads, fc_error, query, gram_inverse, vec_in, fc_master, fc_momentum
    )
    new_error, new_momentum, new_master, new_weights = update(
        merged, base.reshape(merged.shape), basis, col, fc_master, fc_momentum
    )
    vec_out = vec_out.reshape(2, padded)
    vec_weights = (vec_out[1, :length] - approx_scale / n * vec_out[0, :length]).astype(
        jnp.bfloat16
    )
    vec_mean = lax.dynamic_slice_in_dim(vec_out[0], replica * shard, shard, 0) / n
    vec_new_momentum = momentum_decay * vec_momentum + vec_mean
    vec_new_master = vec_master - step_size * (vec_mean + momentum_decay * vec_new_momentum)
    return (
        new_error,
        new_momentum,
        new_master,
        new_weights,
        vec_new_momentum,
        vec_new_master,
        vec_weights,
    )


def solution(mesh):
    return jax.shard_map(
        functools.partial(on_device, mesh.shape["dp"], mesh.shape["tensor"]),
        mesh=mesh,
        in_specs=(
            P("dp", None, "tensor"),
            P("dp", None, "tensor"),
            P("tensor", None),
            P(),
            P("dp", "tensor"),
            P("dp", "tensor"),
            P("dp", None),
            P("dp"),
            P("dp"),
        ),
        out_specs=(
            P("dp", None, "tensor"),
            P("dp", "tensor"),
            P("dp", "tensor"),
            P(None, "tensor"),
            P("dp"),
            P("dp"),
            P(),
        ),
        check_vma=False,
    )
```

time: 425 us -> 73.8 us (0.17)
  waiting for transfers between devices: 241 us -> 0 us
  blocking collectives: 147 us -> 0 us
  Pallas kernels: 0 us -> 62.5 us
  matrix products: 17.6 us -> 0 us
  between operations: 14.5 us -> 0.73 us
    psum x2 -> x0, waiting for transfers between devices: 240 us -> none  [the longest x1 133 us: on_device(): row_total = lax.psum(row_part, ('dp', 'tensor'))]
    psum x1 -> x0, blocking collectives: 75.4 us -> none  [on_device(): vec_total = lax.psum(vec_term, 'dp')]
    unnamed x1 -> x0, blocking collectives: 71.8 us -> none
    pallas_call x0 -> x2, Pallas kernels: none -> 62.5 us  [the longest x1 58.1 us: exchange(): pl.pallas_call(functools.partial(exchange_kernel, n, cores), out_shape=(j...]
    dot_general x5 -> x0, matrix products: 17.6 us -> none  [the longest x1 6.63 us: on_device(): approx = jnp.dot(row_basis, col_mean.T, precision=lax.Precision.HIGHEST)]
  transfers between devices with their start and end apart: 3 -> 0, of which waited for: 2 -> 0; matrix products, arithmetic and copies ran while one was open for 2% -> 0% of each run, Pallas kernels for 0% -> 0%
where the time goes in v1:
time: 73.8 us; the launch traced here: 73.4 us
  Pallas kernels  62.5 us (85%)
  local copies, waits for them, and re-layouts  7.22 us (10%)
  other arithmetic  2.97 us (4%)
    pallas_call x1, Pallas kernels, exchange(): pl.pallas_call(functools.partial(exchange_kernel, n, cores), out_shape=(j...  58.1 us
    unnamed x19, local copies, waits for them, and re-layouts  7.17 us
    pallas_call x1, Pallas kernels, update(): pl.pallas_call(functools.partial(update_kernel, rows_step), grid=(steps,)...  4.4 us

profile of v1, /device:TPU:0, one launch (start us, length us, event | category | flops | bytes accessed | tf_op | source)
XLA Modules:
  0.0 73.4 jit_solution(7154809289624926524)
XLA Ops:
  0.6 0.8 %reduce = bf16[5376]{0:T(1024)(128)(2,1)S(1)} reduce(bf16[1,5376]{1,0:T(2,128)(2,1)} %param.15, bf16[]{:T(256)} %constant.35), dimensions={0}, to_apply=%param.15.reduce_sub_computation | reduce | bytes 21506 | tf_op args[6]
  1.5 0.8 %subtract_dynamic-update-slice_fusion = f32[6144]{0:T(1024)S(1)} fusion(f32[6144]{0:T(1024)S(1)} %broadcast_in_dim.3, s32[]{:T(128)S(6)} %select_n.4, f32[336]{0:T(512)} %param.16, f32[336]{0:T(512)} %param.17), kind=kLoop, calls=%fused_computation.7 | loop fusion | flops 672 | bytes 4740 | tf_op jit(solution)/shard_map/dynamic_update_slice | solution.py:465
  2.3 1.2 %copy.16.query = f32[1536,32]{1,0:T(8,128)S(1)} copy(f32[1536,32]{0,1:T(8,128)} %param.11) | data formatting | bytes 393216 | tf_op args[2]
  3.5 0.0 copy-start
  3.5 1.7 %copy-done = bf16[1,768,1536]{2,1,0:T(8,128)(2,1)S(1)} copy-done((bf16[1,768,1536]{2,1,0:T(8,128)(2,1)S(1)}, bf16[1,768,1536]{2,1,0:T(8,128)(2,1)}, u32[]{:S(2)}) %copy-start) | copy-done | bytes 2359320
  5.2 0.0 copy-start.1
  5.2 1.7 %copy-done.1 = bf16[1,768,1536]{2,1,0:T(8,128)(2,1)S(1)} copy-done((bf16[1,768,1536]{2,1,0:T(8,128)(2,1)S(1)}, bf16[1,768,1536]{2,1,0:T(8,128)(2,1)}, u32[]{:S(2)}) %copy-start.1) | copy-done | bytes 2359320
  6.8 0.0 copy-start.2
  6.8 1.0 %copy-done.2 = f32[48,1536]{1,0:T(8,128)S(1)} copy-done((f32[48,1536]{1,0:T(8,128)S(1)}, f32[48,1536]{1,0:T(8,128)}, u32[]{:S(2)}) %copy-start.2) | copy-done | bytes 294936
  7.8 0.0 copy-start.4
  7.8 1.0 %copy-done.4 = f32[48,1536]{1,0:T(8,128)S(1)} copy-done((f32[48,1536]{1,0:T(8,128)S(1)}, f32[48,1536]{1,0:T(8,128)}, u32[]{:S(2)}) %copy-start.4) | copy-done | bytes 294936
  8.8 0.0 copy-start.6
  8.8 0.7 copy-done.6
  9.5 0.0 copy-start.3
  9.5 0.0 copy-start.5
  9.5 58.1 %exchange.1 = (bf16[768,1536]{1,0:T(8,128)(2,1)S(1)}, bf16[16,48,1536]{2,1,0:T(8,128)(2,1)S(1)}, bf16[768,128]{1,0:T(8,128)(2,1)S(1)}, bf16[128,1536]{1,0:T(8,128)(2,1)S(1)}, f32[6,16,128]{2,1,0:T(8,128)S(1)}) custom-call(bf16[1,768,1536]{2,1,0:T(8,128)(2,1)S(1)} %copy-done, bf16[1,768,1536]{2,1,0:T(8,128)(2,1)S(1)} %copy-done.1, ...), custom_call_target="tpu_custom_call" | custom-call | flops 150994944 | bytes 14000000 | tf_op jit(solution)/shard_map/exchange/pallas_call | solution.py:340
  67.6 0.0 copy-done.3
  67.6 0.0 copy-done.5
  67.6 0.0 copy-start.7
  67.6 0.0 copy-start.8
  67.6 4.4 %update.1 = (bf16[1,768,1536]{2,1,0:T(8,128)(2,1)}, f32[48,1536]{1,0:T(8,128)}, f32[48,1536]{1,0:T(8,128)}, bf16[768,1536]{1,0:T(8,128)(2,1)}) custom-call(bf16[768,1536]{1,0:T(8,128)(2,1)S(1)} %get-tuple-element.16.merged, bf16[768,1536]{1,0:T(8,128)(2,1)S(1)} %bitcast.5, bf16[768,128]{1,0:T(8,128)(2,1)S(1)} %get-tuple-element.18.basis, ...), custom_call_target="tpu_custom_call" | custom-call | tf_op jit(solution)/shard_map/update/pallas_call | solution.py:427
  72.1 0.7 convert_reduce_fusion
  72.7 0.0 copy-done.7
  72.7 0.0 copy-done.8
  72.7 0.7 multiply_subtract_fusion
  (6 shorter events, 0.1 us)
Async XLA Ops:
  3.5 1.7 %copy-start = (bf16[1,768,1536]{2,1,0:T(8,128)(2,1)S(1)}, bf16[1,768,1536]{2,1,0:T(8,128)(2,1)}, u32[]{:S(2)}) copy-start(bf16[1,768,1536]{2,1,0:T(8,128)(2,1)} %grads.1) | copy-start | bytes 7077892
  5.2 1.7 %copy-start.1 = (bf16[1,768,1536]{2,1,0:T(8,128)(2,1)S(1)}, bf16[1,768,1536]{2,1,0:T(8,128)(2,1)}, u32[]{:S(2)}) copy-start(bf16[1,768,1536]{2,1,0:T(8,128)(2,1)} %error.1) | copy-start | bytes 7077892
  6.8 1.0 %copy-start.2 = (f32[48,1536]{1,0:T(8,128)S(1)}, f32[48,1536]{1,0:T(8,128)}, u32[]{:S(2)}) copy-start(f32[48,1536]{1,0:T(8,128)} %master.3) | copy-start | bytes 884740
  7.8 1.0 %copy-start.4 = (f32[48,1536]{1,0:T(8,128)S(1)}, f32[48,1536]{1,0:T(8,128)}, u32[]{:S(2)}) copy-start(f32[48,1536]{1,0:T(8,128)} %momentum.3) | copy-start | bytes 884740
  8.8 0.7 copy-start.6
  9.5 58.1 %copy-start.3 = (f32[48,1536]{1,0:T(8,128)S(1)}, f32[48,1536]{1,0:T(8,128)}, u32[]{:S(2)}) copy-start(f32[48,1536]{1,0:T(8,128)} %master.3) | copy-start | bytes 884740
  9.5 58.1 %copy-start.5 = (f32[48,1536]{1,0:T(8,128)S(1)}, f32[48,1536]{1,0:T(8,128)}, u32[]{:S(2)}) copy-start(f32[48,1536]{1,0:T(8,128)} %momentum.3) | copy-start | bytes 884740
  67.6 5.1 %copy-start.7 = (f32[336]{0:T(512)S(1)}, f32[336]{0:T(512)}, u32[]{:S(2)}) copy-start(f32[336]{0:T(512)} %param.16) | copy-start | bytes 4036
  67.6 5.1 %copy-start.8 = (f32[336]{0:T(512)S(1)}, f32[336]{0:T(512)}, u32[]{:S(2)}) copy-start(f32[336]{0:T(512)} %param.17) | copy-start | bytes 4036

commit v2 on v1

--- a/solution.py
+++ b/solution.py
@@ -39,9 +39,10 @@
     cores,
     grads,
     error,
-    query,
+    query_t,
     gram,
-    vec_in,
+    vec_grads,
+    vec_base,
     master,
     momentum,
     merged_out,
@@ -51,6 +52,10 @@
     vec_out,
     grads_v,
     error_v,
+    query_v,
+    gram_v,
+    master_v,
+    momentum_v,
     merged,
     own_base,
     part,
@@ -60,6 +65,7 @@
     col_in,
     col_total,
     load_sem,
+    small_sem,
     out_sem,
     part_send,
     part_recv,
@@ -71,17 +77,31 @@
     ctotal_recv,
     base_send,
     line_recv,
-    plane_recv,
+    x_recv,
+    y_recv,
+    corner_recv,
 ):
     rows_all, columns = merged.shape
     blocks = rows_all // ROW_BLOCK
     row_chunks = 2 * blocks
     chunks = part.shape[0]
+    vec_chunks = (chunks - row_chunks) // 2
     devices = n * cores
     me, core = lax.axis_index("dp"), lax.axis_index("tensor")
     flat = core * n + me
     outer = n // INNER
     o, i = lax.div(me, INNER), lax.rem(me, INNER)
+    ix = i + 1 - 2 * lax.rem(i, 2)
+    iy = lax.rem(i + 2, INNER)
+
+    small = [
+        pltpu.make_async_copy(src, dst, small_sem.at[k])
+        for k, (src, dst) in enumerate(
+            ((master, master_v), (momentum, momentum_v), (query_t, query_v), (gram, gram_v))
+        )
+    ]
+    for copy in small:
+        copy.start()
 
     def load(b):
         rows = pl.ds(pl.multiple_of(b * ROW_BLOCK, ROW_BLOCK), ROW_BLOCK)
@@ -105,30 +125,74 @@
 
     lax.fori_loop(1, devices, greet, 0)
 
-    own_base[...] = (master[...] - base_decay * momentum[...]).astype(jnp.bfloat16)
-    query_t = query[...].T.astype(jnp.bfloat16)
-    part[row_chunks:] = vec_in[...]
+    vec = vec_grads[...].astype(jnp.float32) * (core == 0).astype(jnp.float32)
+    lanes = [vec[:, k : k + 128] for k in range(0, vec.shape[1], 128)]
+    lanes += [jnp.zeros((1, 128), jnp.float32)] * (16 * vec_chunks - len(lanes))
+    for k in range(vec_chunks):
+        part[row_chunks + k] = jnp.concatenate(lanes[16 * k : 16 * k + 16], axis=0)
+    part[row_chunks + vec_chunks :] = vec_base[...]
+    small[0].wait()
+    small[1].wait()
+    own_base[...] = (master_v[...] - base_decay * momentum_v[...]).astype(jnp.bfloat16)
+    small[2].wait()
+    small[3].wait()
+    query_b = query_v[...].astype(jnp.bfloat16)
 
     pl.semaphore_wait(barrier, devices - 1)
 
     keep = pltpu.make_async_copy(own_base, base_all.at[me], out_sem.at[0])
     keep.start()
 
-    def send_line(t, carry):
-        o2 = lax.rem(o + t, outer)
-        remote(
-            own_base, base_all.at[me], base_send, line_recv.at[o], o2 * INNER + i, core
-        ).start()
-        return carry
-
-    lax.fori_loop(1, outer, send_line, 0)
-
-    def send_plane(s, carry):
-        i2 = lax.rem(i + s, INNER)
-        remote(own_base, base_all.at[me], base_send, plane_recv, o * INNER + i2, core).start()
-        return carry
-
-    lax.fori_loop(1, INNER, send_plane, 0)
+    def send_block(src, slot, o2, i2, recv_sem):
+        remote(src, base_all.at[slot], base_send, recv_sem, o2 * INNER + i2, core).start()
+
+    pl.when(o + 1 < outer)(lambda: send_block(own_base, me, o + 1, i, line_recv.at[o]))
+    pl.when(o >= 1)(lambda: send_block(own_base, me, o - 1, i, line_recv.at[o]))
+    send_block(own_base, me, o, ix, x_recv.at[o])
+    send_block(own_base, me, o, iy, y_recv.at[o])
+
+    def line_step(d):
+        for side in (-1, 1):
+            o2 = o + side * d
+
+            @pl.when(jnp.logical_and(o2 >= 0, o2 < outer))
+            def _(o2=o2, side=side):
+                slot = o2 * INNER + i
+                src = base_all.at[slot]
+                wait_bytes(src, line_recv.at[o2])
+                o3 = o - side
+                pl.when(jnp.logical_and(o3 >= 0, o3 < outer))(
+                    lambda: send_block(src, slot, o3, i, line_recv.at[o2])
+                )
+                send_block(src, slot, o, ix, x_recv.at[o2])
+                send_block(src, slot, o, iy, y_recv.at[o2])
+
+    def corner_step(d):
+        for side in (-1, 1) if d else (1,):
+            o2 = o + side * d
+            by_x = d % 4 == 0 or (d % 4 == 1 and side < 0) or (d % 4 == 3 and side > 0)
+
+            @pl.when(jnp.logical_and(o2 >= 0, o2 < outer))
+            def _(o2=o2, by_x=by_x):
+                slot_x, slot_y = o2 * INNER + ix, o2 * INNER + iy
+                if by_x:
+                    wait_bytes(base_all.at[slot_x], x_recv.at[o2])
+                    send_block(base_all.at[slot_x], slot_x, o, iy, corner_recv)
+                else:
+                    wait_bytes(base_all.at[slot_y], y_recv.at[o2])
+                    send_block(base_all.at[slot_y], slot_y, o, ix, corner_recv)
+
+    def finish_step(d):
+        for side in (-1, 1) if d else (1,):
+            o2 = o + side * d
+            by_x = d % 4 == 0 or (d % 4 == 1 and side < 0) or (d % 4 == 3 and side > 0)
+
+            @pl.when(jnp.logical_and(o2 >= 0, o2 < outer))
+            def _(o2=o2, by_x=by_x):
+                if by_x:
+                    wait_bytes(base_all.at[o2 * INNER + iy], y_recv.at[o2])
+                else:
+                    wait_bytes(base_all.at[o2 * INNER + ix], x_recv.at[o2])
 
     def send_part(k):
         mine = flat == k
@@ -158,7 +222,7 @@
         ).astype(jnp.bfloat16)
         merged[rows, :] = block
         term = lax.dot_general(
-            query_t, block, (((1,), (1,)), ((), ())), preferred_element_type=jnp.float32
+            query_b, block, (((1,), (1,)), ((), ())), preferred_element_type=jnp.float32
         )
         part[pl.ds(2 * b, 1)] = term[None, :16]
         part[pl.ds(2 * b + 1, 1)] = term[None, 16:]
@@ -169,6 +233,8 @@
     lax.fori_loop(0, blocks, row_step, 0)
     keep_merged = pltpu.make_async_copy(merged, merged_out, out_sem.at[1])
     keep_merged.start()
+
+    line_step(1)
 
     owner = flat < chunks
 
@@ -190,11 +256,13 @@
             return carry
 
         lax.fori_loop(1, devices, spread, 0)
-        wait_bytes(total.at[pl.ds(0, chunks - 1)], total_recv)
-
-    @pl.when(jnp.logical_not(owner))
-    def _():
-        wait_bytes(total.at[pl.ds(0, chunks)], total_recv)
+
+    corner_step(0)
+    if outer > 2:
+        line_step(2)
+
+    pl.when(owner)(lambda: wait_bytes(total.at[pl.ds(0, chunks - 1)], total_recv))
+    pl.when(jnp.logical_not(owner))(lambda: wait_bytes(total.at[pl.ds(0, chunks)], total_recv))
 
     row_mean = (
         jnp.concatenate(
@@ -207,7 +275,7 @@
         / n
     )
     basis = jnp.dot(
-        gram[...].T,
+        gram_v[...].T,
         row_mean,
         precision=lax.Precision.HIGHEST,
         preferred_element_type=jnp.float32,
@@ -235,26 +303,9 @@
                     col_part.at[k], col_in.at[me], cpart_send, cpart_recv, k, core
                 ).start()
 
-    def relay(t, carry):
-        o2 = lax.rem(o + outer - t, outer)
-        slot = o2 * INNER + i
-        wait_bytes(base_all.at[slot], line_recv.at[o2])
-
-        def hand(s, inner_carry):
-            i2 = lax.rem(i + s, INNER)
-            remote(
-                base_all.at[slot],
-                base_all.at[slot],
-                base_send,
-                plane_recv,
-                o * INNER + i2,
-                core,
-            ).start()
-            return inner_carry
-
-        return lax.fori_loop(1, INNER, hand, carry)
-
-    lax.fori_loop(1, outer, relay, 0)
+    for d in range(3, outer):
+        line_step(d)
+    corner_step(1)
 
     high = basis_b.astype(jnp.float32)
     low = basis - high
@@ -277,16 +328,25 @@
             return carry
 
         lax.fori_loop(1, n, spread, 0)
-        wait_bytes(col_total.at[pl.ds(0, COL_OWNERS - 1)], ctotal_recv)
-
-    if n == COL_OWNERS:
+
+    everyone_owns = n == COL_OWNERS
+    if everyone_owns:
         col_owner()
     else:
         pl.when(me < COL_OWNERS)(col_owner)
 
-        @pl.when(me >= COL_OWNERS)
-        def _():
-            wait_bytes(col_total.at[pl.ds(0, COL_OWNERS)], ctotal_recv)
+    for d in range(2, outer):
+        corner_step(d)
+
+    if everyone_owns:
+        wait_bytes(col_total.at[pl.ds(0, COL_OWNERS - 1)], ctotal_recv)
+    else:
+        pl.when(me < COL_OWNERS)(
+            lambda: wait_bytes(col_total.at[pl.ds(0, COL_OWNERS - 1)], ctotal_recv)
+        )
+        pl.when(me >= COL_OWNERS)(
+            lambda: wait_bytes(col_total.at[pl.ds(0, COL_OWNERS)], ctotal_recv)
+        )
 
     for c in range(4):
         col_mean = jnp.concatenate([col_total[4 * c + r] for r in range(4)], axis=0) / n
@@ -312,29 +372,36 @@
         wait_bytes(col_part.at[pl.ds(0, COL_OWNERS - 1)], cpart_send)
         wait_bytes(col_in.at[pl.ds(0, n - 1)], ctotal_send)
 
-    if n == COL_OWNERS:
+    if everyone_owns:
         col_sent()
     else:
         pl.when(me < COL_OWNERS)(col_sent)
-
-        @pl.when(me >= COL_OWNERS)
-        def _():
-            wait_bytes(col_part.at[pl.ds(0, COL_OWNERS)], cpart_send)
-
-    wait_bytes(base_all.at[pl.ds(0, (INNER - 1) * outer)], plane_recv)
-    wait_bytes(base_all.at[pl.ds(0, n - 1)], base_send)
-
-
-def exchange(n, cores, grads, error, query, gram, vec_in, master, momentum):
+        pl.when(me >= COL_OWNERS)(
+            lambda: wait_bytes(col_part.at[pl.ds(0, COL_OWNERS)], cpart_send)
+        )
+
+    for d in range(outer):
+        finish_step(d)
+    wait_bytes(base_all.at[pl.ds(0, outer)], corner_recv)
+    wait_bytes(base_all.at[pl.ds(0, 3 * outer)], base_send)
+    ends = jnp.logical_or(o == 0, o == outer - 1)
+    pl.when(ends)(lambda: wait_bytes(base_all.at[pl.ds(0, 1)], base_send))
+    pl.when(jnp.logical_not(ends))(
+        lambda: wait_bytes(base_all.at[pl.ds(0, outer + 1)], base_send)
+    )
+
+
+def exchange(n, cores, grads, error, query_t, gram, vec_grads, vec_base, master, momentum):
     rows_all, columns = grads.shape[1:]
-    rank = query.shape[1]
+    rank = query_t.shape[0]
     rows = master.shape[0]
     blocks = rows_all // ROW_BLOCK
-    chunks = 2 * blocks + vec_in.shape[0]
+    chunks = 2 * (blocks + vec_base.shape[0])
     wide = columns // 4
     devices = n * cores
     vmem = pl.BlockSpec(memory_space=pltpu.VMEM)
-    hbm = pl.BlockSpec(memory_space=pl.ANY)
+    anywhere = pl.BlockSpec(memory_space=pl.ANY)
+    hbm = pl.BlockSpec(memory_space=pltpu.HBM)
     dma = pltpu.SemaphoreType.DMA
     f32, bf16 = jnp.float32, jnp.bfloat16
     return pl.pallas_call(
@@ -344,13 +411,17 @@
             jax.ShapeDtypeStruct((n, rows, columns), bf16),
             jax.ShapeDtypeStruct((rows_all, 4 * rank), bf16),
             jax.ShapeDtypeStruct((4 * rank, columns), bf16),
-            jax.ShapeDtypeStruct(vec_in.shape, f32),
+            jax.ShapeDtypeStruct((2 * vec_base.shape[0],) + vec_base.shape[1:], f32),
         ),
-        in_specs=[hbm, hbm, vmem, vmem, vmem, vmem, vmem],
-        out_specs=(hbm, hbm, vmem, vmem, vmem),
+        in_specs=[hbm, hbm, hbm, hbm, vmem, vmem, hbm, hbm],
+        out_specs=(anywhere, anywhere, vmem, vmem, vmem),
         scratch_shapes=[
             pltpu.VMEM((rows_all, columns), bf16),
             pltpu.VMEM((rows_all, columns), bf16),
+            pltpu.VMEM(query_t.shape, f32),
+            pltpu.VMEM(gram.shape, f32),
+            pltpu.VMEM(master.shape, f32),
+            pltpu.VMEM(master.shape, f32),
             pltpu.VMEM((rows_all, columns), bf16),
             pltpu.VMEM((rows, columns), bf16),
             pltpu.VMEM((chunks, 16, 128), f32),
@@ -360,10 +431,12 @@
             pltpu.VMEM((n, 8, wide), f32),
             pltpu.VMEM((COL_OWNERS, 8, wide), f32),
             dma((blocks, 2)),
+            dma((4,)),
             dma((2,)),
         ]
-        + [dma] * 8
-        + [dma, dma((n // INNER,)), dma],
+        + [dma] * 9
+        + [dma((n // INNER,))] * 3
+        + [dma],
         compiler_params=pltpu.CompilerParams(
             collective_id=0, has_side_effects=True, vmem_limit_bytes=VMEM_LIMIT
         ),
@@ -371,7 +444,7 @@
             flops=4 * rows_all * columns * rank, bytes_accessed=14000000, transcendentals=0
         ),
         name="exchange",
-    )(grads, error, query, gram, vec_in, master, momentum)
+    )(grads, error, query_t, gram, vec_grads, vec_base, master, momentum)
 
 
 def update_kernel(
@@ -460,19 +533,26 @@
 ):
     replica = lax.axis_index("dp")
     length, shard = vec_grads.shape[1], vec_master.shape[0]
-    counts = (lax.axis_index("tensor") == 0).astype(jnp.float32)
+    counts = lax.axis_index("tensor") == 0
     padded = -(-length // 2048) * 2048
     vec_base = lax.dynamic_update_slice_in_dim(
         jnp.zeros((padded,), jnp.float32),
-        vec_master - base_decay * vec_momentum,
+        jnp.where(counts, vec_master - base_decay * vec_momentum, 0.0),
         replica * shard,
         0,
-    )
-    vec_sum = jnp.pad(vec_grads[0].astype(jnp.float32), (0, padded - length))
-    vec_in = (counts * jnp.concatenate([vec_sum, vec_base])).reshape(-1, 16, 128)
+    ).reshape(-1, 16, 128)
 
     merged, base, basis, col, vec_out = exchange(
-        n, cores, fc_grads, fc_error, query, gram_inverse, vec_in, fc_master, fc_momentum
+        n,
+        cores,
+        fc_grads,
+        fc_error,
+        query.T,
+        gram_inverse,
+        vec_grads,
+        vec_base,
+        fc_master,
+        fc_momentum,
     )
     new_error, new_momentum, new_master, new_weights = update(
         merged, base.reshape(merged.shape), basis, col, fc_master, fc_momentum

time: 73.8 us -> 56.6 us (0.77)
  Pallas kernels: 62.5 us -> 45.6 us
  other arithmetic: 2.97 us -> 2.16 us
    pallas_call x1, Pallas kernels: 58.1 us -> 41.2 us  [exchange(): pl.pallas_call(functools.partial(exchange_kernel, n, cores), out_shape=(j...]
    unnamed x1 -> x0, other arithmetic: 0.8 us -> none
    unnamed x19 -> x20, local copies, waits for them, and re-layouts: 7.17 us -> 7.64 us
where the time goes in v2:
time: 56.6 us; the launch traced here: 56.2 us
  Pallas kernels  45.6 us (81%)
  local copies, waits for them, and re-layouts  7.67 us (14%)
  other arithmetic  2.16 us (4%)
  between operations  0.69 us (1%)
    pallas_call x1, Pallas kernels, exchange(): pl.pallas_call(functools.partial(exchange_kernel, n, cores), out_shape=(j...  41.2 us
    unnamed x20, local copies, waits for them, and re-layouts  7.64 us
    pallas_call x1, Pallas kernels, update(): pl.pallas_call(functools.partial(update_kernel, rows_step), grid=(steps,)...  4.4 us

profile of v2, /device:TPU:0, one launch (start us, length us, event | category | flops | bytes accessed | tf_op | source)
XLA Modules:
  0.0 56.2 jit_solution(14017735076602712867)
XLA Ops:
  0.7 0.8 %select_dynamic-update-slice_fusion = f32[6144]{0:T(1024)S(1)} fusion(f32[6144]{0:T(1024)S(1)} %broadcast_in_dim.7, s32[]{:T(128)S(6)} %select_n.14, f32[336]{0:T(512)} %param.16, f32[336]{0:T(512)} %param.17, pred[]{:T(512)S(6)} %eq.3), kind=kLoop, calls=%fused_computation.6 | loop fusion | flops 1008 | bytes 4741 | tf_op jit(solution)/shard_map/dynamic_update_slice | solution.py:538
  1.5 0.0 copy-start
  1.5 1.7 %copy-done = bf16[1,768,1536]{2,1,0:T(8,128)(2,1)S(1)} copy-done((bf16[1,768,1536]{2,1,0:T(8,128)(2,1)S(1)}, bf16[1,768,1536]{2,1,0:T(8,128)(2,1)}, u32[]{:S(2)}) %copy-start) | copy-done | bytes 2359320
  3.1 0.0 copy-start.1
  3.1 1.7 %copy-done.1 = bf16[1,768,1536]{2,1,0:T(8,128)(2,1)S(1)} copy-done((bf16[1,768,1536]{2,1,0:T(8,128)(2,1)S(1)}, bf16[1,768,1536]{2,1,0:T(8,128)(2,1)}, u32[]{:S(2)}) %copy-start.1) | copy-done | bytes 2359320
  4.8 0.0 copy-start.2
  4.8 1.0 %copy-done.2 = f32[48,1536]{1,0:T(8,128)S(1)} copy-done((f32[48,1536]{1,0:T(8,128)S(1)}, f32[48,1536]{1,0:T(8,128)}, u32[]{:S(2)}) %copy-start.2) | copy-done | bytes 294936
  5.8 0.0 copy-start.3
  5.8 1.0 %copy-done.3 = f32[48,1536]{1,0:T(8,128)S(1)} copy-done((f32[48,1536]{1,0:T(8,128)S(1)}, f32[48,1536]{1,0:T(8,128)}, u32[]{:S(2)}) %copy-start.3) | copy-done | bytes 294936
  6.7 0.0 copy-start.5
  6.7 0.9 %copy-done.5 = f32[1536,32]{0,1:T(8,128)S(1)} copy-done((f32[1536,32]{0,1:T(8,128)S(1)}, f32[1536,32]{0,1:T(8,128)}, u32[]{:S(2)}) %copy-start.5) | copy-done | bytes 196632
  7.7 0.0 copy-start.6
  7.7 0.7 %copy-done.6 = bf16[1,5376]{1,0:T(2,128)(2,1)S(1)} copy-done((bf16[1,5376]{1,0:T(2,128)(2,1)S(1)}, bf16[1,5376]{1,0:T(2,128)(2,1)}, u32[]{:S(2)}) %copy-start.6) | copy-done | bytes 10776
  8.4 0.0 copy-start.7
  8.4 0.7 %copy-done.7 = f32[32,32]{1,0:T(8,128)S(1)} copy-done((f32[32,32]{1,0:T(8,128)S(1)}, f32[32,32]{1,0:T(8,128)}, u32[]{:S(2)}) %copy-start.7) | copy-done | bytes 4120
  9.1 0.0 copy-start.4
  9.1 41.2 %exchange.1 = (bf16[768,1536]{1,0:T(8,128)(2,1)S(1)}, bf16[16,48,1536]{2,1,0:T(8,128)(2,1)S(1)}, bf16[768,128]{1,0:T(8,128)(2,1)S(1)}, bf16[128,1536]{1,0:T(8,128)(2,1)S(1)}, f32[6,16,128]{2,1,0:T(8,128)S(1)}) custom-call(bf16[1,768,1536]{2,1,0:T(8,128)(2,1)S(1)} %copy-done, bf16[1,768,1536]{2,1,0:T(8,128)(2,1)S(1)} %copy-done.1, f32[32,1536]{1,0:T(8,128)S(1)} %bitcast.5, ...), custom_call_target="tpu_custom_call" | custom-call | flops 150994944 | bytes 14000000 | tf_op jit(solution)/shard_map/exchange/pallas_call | solution.py:407
  50.4 0.0 copy-done.4
  50.4 0.0 copy-start.8
  50.4 0.0 copy-start.9
  50.4 4.4 %update.1 = (bf16[1,768,1536]{2,1,0:T(8,128)(2,1)}, f32[48,1536]{1,0:T(8,128)}, f32[48,1536]{1,0:T(8,128)}, bf16[768,1536]{1,0:T(8,128)(2,1)}) custom-call(bf16[768,1536]{1,0:T(8,128)(2,1)S(1)} %get-tuple-element.16.merged, bf16[768,1536]{1,0:T(8,128)(2,1)S(1)} %bitcast.4, bf16[768,128]{1,0:T(8,128)(2,1)S(1)} %get-tuple-element.18.basis, ...), custom_call_target="tpu_custom_call" | custom-call | tf_op jit(solution)/shard_map/update/pallas_call | solution.py:500
  54.8 0.7 %convert_reduce_fusion = bf16[5376]{0:T(1024)(128)(2,1)} fusion(f32[2,6144]{1,0:T(2,128)S(1)} %reshape.31), kind=kLoop, calls=%fused_computation.2 | loop fusion | flops 16128 | bytes 53760 | tf_op jit(solution)/shard_map/convert_element_type | solution.py:561
  55.5 0.0 copy-done.8
  55.5 0.0 copy-done.9
  55.5 0.7 %multiply_subtract_fusion = (f32[336]{0:T(512)}, f32[336]{0:T(512)}) fusion(f32[336]{0:T(512)S(1)} %copy-done.8, f32[6144]{0:T(1024)S(1)} %bitcast.7, s32[]{:T(128)S(6)} %select_n.14, f32[336]{0:T(512)S(1)} %copy-done.9), kind=kLoop, calls=%fused_computation.3 | loop fusion | flops 2352 | bytes 6724 | tf_op jit(solution)/shard_map/sub | solution.py:566
  (3 shorter events, 0.0 us)
Async XLA Ops:
  1.5 1.7 %copy-start = (bf16[1,768,1536]{2,1,0:T(8,128)(2,1)S(1)}, bf16[1,768,1536]{2,1,0:T(8,128)(2,1)}, u32[]{:S(2)}) copy-start(bf16[1,768,1536]{2,1,0:T(8,128)(2,1)} %grads.1) | copy-start | bytes 7077892
  3.1 1.7 %copy-start.1 = (bf16[1,768,1536]{2,1,0:T(8,128)(2,1)S(1)}, bf16[1,768,1536]{2,1,0:T(8,128)(2,1)}, u32[]{:S(2)}) copy-start(bf16[1,768,1536]{2,1,0:T(8,128)(2,1)} %error.1) | copy-start | bytes 7077892
  4.8 1.0 %copy-start.2 = (f32[48,1536]{1,0:T(8,128)S(1)}, f32[48,1536]{1,0:T(8,128)}, u32[]{:S(2)}) copy-start(f32[48,1536]{1,0:T(8,128)} %master.3) | copy-start | bytes 884740
  5.8 1.0 %copy-start.3 = (f32[48,1536]{1,0:T(8,128)S(1)}, f32[48,1536]{1,0:T(8,128)}, u32[]{:S(2)}) copy-start(f32[48,1536]{1,0:T(8,128)} %momentum.3) | copy-start | bytes 884740
  6.7 0.9 %copy-start.5 = (f32[1536,32]{0,1:T(8,128)S(1)}, f32[1536,32]{0,1:T(8,128)}, u32[]{:S(2)}) copy-start(f32[1536,32]{0,1:T(8,128)} %param.11) | copy-start | bytes 589828
  7.7 0.7 %copy-start.6 = (bf16[1,5376]{1,0:T(2,128)(2,1)S(1)}, bf16[1,5376]{1,0:T(2,128)(2,1)}, u32[]{:S(2)}) copy-start(bf16[1,5376]{1,0:T(2,128)(2,1)} %vec_grads.1) | copy-start | bytes 32260
  8.4 0.7 %copy-start.7 = (f32[32,32]{1,0:T(8,128)S(1)}, f32[32,32]{1,0:T(8,128)}, u32[]{:S(2)}) copy-start(f32[32,32]{1,0:T(8,128)} %gram.1) | copy-start | bytes 12292
  9.1 41.2 %copy-start.4 = (f32[48,1536]{1,0:T(8,128)S(1)}, f32[48,1536]{1,0:T(8,128)}, u32[]{:S(2)}) copy-start(f32[48,1536]{1,0:T(8,128)} %momentum.3) | copy-start | bytes 884740
  50.4 5.1 %copy-start.8 = (f32[336]{0:T(512)S(1)}, f32[336]{0:T(512)}, u32[]{:S(2)}) copy-start(f32[336]{0:T(512)} %param.16) | copy-start | bytes 4036
  50.4 5.1 %copy-start.9 = (f32[336]{0:T(512)S(1)}, f32[336]{0:T(512)}, u32[]{:S(2)}) copy-start(f32[336]{0:T(512)} %param.17) | copy-start | bytes 4036

commit v3 on v2

--- a/solution.py
+++ b/solution.py
@@ -16,7 +16,7 @@
 INNER = 4
 ROW_BLOCK = 128
 COL_OWNERS = 16
-VMEM_LIMIT = 40 * 1024 * 1024
+VMEM_LIMIT = 60 * 1024 * 1024
 
 
 def remote(src, dst, send_sem, recv_sem, dp, core):

time: 56.6 us -> 51.9 us (0.917)
  local copies, waits for them, and re-layouts: 7.67 us -> 0.66 us
  Pallas kernels: 45.6 us -> 48 us
    unnamed x20 -> x8, local copies, waits for them, and re-layouts: 7.64 us -> 0.62 us
    pallas_call x1, Pallas kernels: 4.4 us -> 7.57 us  [update(): pl.pallas_call(functools.partial(update_kernel, rows_step), grid=(steps,)...]
    pallas_call x1, Pallas kernels: 41.2 us -> 40.4 us  [exchange(): pl.pallas_call(functools.partial(exchange_kernel, n, cores), out_shape=(j...]
where the time goes in v3:
time: 51.9 us; the launch traced here: 51.5 us
  Pallas kernels  48 us (92%)
  other arithmetic  2.16 us (4%)
  between operations  0.7 us (1%)
  local copies, waits for them, and re-layouts  0.66 us (1%)
    pallas_call x1, Pallas kernels, exchange(): pl.pallas_call(functools.partial(exchange_kernel, n, cores), out_shape=(j...  40.4 us
    pallas_call x1, Pallas kernels, update(): pl.pallas_call(functools.partial(update_kernel, rows_step), grid=(steps,)...  7.57 us

profile of v3, /device:TPU:0, one launch (start us, length us, event | category | flops | bytes accessed | tf_op | source)
XLA Modules:
  0.0 51.5 jit_solution(9808139445663592391)
XLA Ops:
  0.7 0.8 %select_dynamic-update-slice_fusion = f32[6144]{0:T(1024)S(1)} fusion(f32[6144]{0:T(1024)S(1)} %broadcast_in_dim.7, s32[]{:T(128)S(6)} %select_n.14, f32[336]{0:T(512)} %param.16, f32[336]{0:T(512)} %param.17, pred[]{:T(512)S(6)} %eq.3), kind=kLoop, calls=%fused_computation.6 | loop fusion | flops 1008 | bytes 4741 | tf_op jit(solution)/shard_map/dynamic_update_slice | solution.py:538
  1.5 0.0 copy-start.1
  1.5 0.6 %copy-done.1 = f32[6144]{0:T(1024)} copy-done((f32[6144]{0:T(1024)}, f32[6144]{0:T(1024)S(1)}, u32[]{:S(2)}) %copy-start.1) | copy-done | bytes 24600
  2.1 40.4 %exchange.1 = (bf16[768,1536]{1,0:T(8,128)(2,1)}, bf16[16,48,1536]{2,1,0:T(8,128)(2,1)}, bf16[768,128]{1,0:T(8,128)(2,1)}, bf16[128,1536]{1,0:T(8,128)(2,1)}, f32[6,16,128]{2,1,0:T(8,128)}) custom-call(bf16[1,768,1536]{2,1,0:T(8,128)(2,1)} %grads.1, bf16[1,768,1536]{2,1,0:T(8,128)(2,1)} %error.1, f32[32,1536]{1,0:T(8,128)} %bitcast.5, f32[32,32]{1,0:T(8,128)} %gram.1, ...), custom_call_target="tpu_custom_call" | custom-call | flops 150994944 | bytes 14000000 | tf_op jit(solution)/shard_map/exchange/pallas_call | solution.py:407
  42.5 0.0 copy-start
  42.5 0.0 copy-start.2
  42.5 0.0 copy-start.3
  42.6 7.6 %update.1 = (bf16[1,768,1536]{2,1,0:T(8,128)(2,1)}, f32[48,1536]{1,0:T(8,128)}, f32[48,1536]{1,0:T(8,128)}, bf16[768,1536]{1,0:T(8,128)(2,1)}) custom-call(bf16[768,1536]{1,0:T(8,128)(2,1)} %get-tuple-element.16.merged, bf16[768,1536]{1,0:T(8,128)(2,1)} %bitcast.4, bf16[768,128]{1,0:T(8,128)(2,1)} %get-tuple-element.18.basis, ...), custom_call_target="tpu_custom_call" | custom-call | tf_op jit(solution)/shard_map/update/pallas_call | solution.py:500
  50.1 0.0 copy-done
  50.2 0.7 %convert_reduce_fusion = bf16[5376]{0:T(1024)(128)(2,1)} fusion(f32[2,6144]{1,0:T(2,128)S(1)} %reshape.31), kind=kLoop, calls=%fused_computation.2 | loop fusion | flops 16128 | bytes 53760 | tf_op jit(solution)/shard_map/convert_element_type | solution.py:561
  50.9 0.0 copy-done.2
  50.9 0.0 copy-done.3
  50.9 0.7 %multiply_subtract_fusion = (f32[336]{0:T(512)}, f32[336]{0:T(512)}) fusion(f32[336]{0:T(512)S(1)} %copy-done.2, f32[6144]{0:T(1024)S(1)} %bitcast.7, s32[]{:T(128)S(6)} %select_n.14, f32[336]{0:T(512)S(1)} %copy-done.3), kind=kLoop, calls=%fused_computation.3 | loop fusion | flops 2352 | bytes 6724 | tf_op jit(solution)/shard_map/sub | solution.py:566
  (3 shorter events, 0.0 us)
Async XLA Ops:
  1.5 0.6 %copy-start.1 = (f32[6144]{0:T(1024)}, f32[6144]{0:T(1024)S(1)}, u32[]{:S(2)}) copy-start(f32[6144]{0:T(1024)S(1)} %select_dynamic-update-slice_fusion) | copy-start | bytes 73732
  42.5 7.6 %copy-start = (f32[6,16,128]{2,1,0:T(8,128)S(1)}, f32[6,16,128]{2,1,0:T(8,128)}, u32[]{:S(2)}) copy-start(f32[6,16,128]{2,1,0:T(8,128)} %get-tuple-element.24) | copy-start | bytes 147460
  42.5 8.3 %copy-start.2 = (f32[336]{0:T(512)S(1)}, f32[336]{0:T(512)}, u32[]{:S(2)}) copy-start(f32[336]{0:T(512)} %param.16) | copy-start | bytes 4036
  42.5 8.3 %copy-start.3 = (f32[336]{0:T(512)S(1)}, f32[336]{0:T(512)}, u32[]{:S(2)}) copy-start(f32[336]{0:T(512)} %param.17) | copy-start | bytes 4036
